TPU v7x, 32 devices: a whole 2x2x4 slice. The times are simulated.
32 devices in a mesh: parts: 2 (over y), tensor: 16 (over z, x, core).
Axes of the slice: x: 2, y: 2, z: 4, core: 2. Of those that a mesh axis runs over, the one named last changes fastest.
Arguments:
- residual_input: bfloat16 [16, 8192], P('parts', 'tensor'), parts along dimension 0, may hold values from -42 to 42
- attention_norm_gain: bfloat16 [8192], P('tensor'), may hold values from 0.25 to 1.75
- wq: bfloat16 [8192, 8192], P('tensor'), may hold values from -0.0625 to 0.0625
- wk: bfloat16 [1024, 8192], P('tensor'), may hold values from -0.0625 to 0.0625
- wv: bfloat16 [1024, 8192], P('tensor'), may hold values from -0.0625 to 0.0625
- wo: bfloat16 [8192, 8192], P('tensor'), may hold values from -0.0625 to 0.0625
- query_down_factor: bfloat16 [32, 8192, 32], P(None, 'tensor'), may hold values from -0.0625 to 0.0625
- query_up_factor: bfloat16 [32, 32, 8192], P(None, None, 'tensor'), may hold values from -1 to 1
- value_down_factor: bfloat16 [32, 8192, 32], P(None, 'tensor'), may hold values from -0.0625 to 0.0625
- value_up_factor: bfloat16 [32, 32, 1024], P(None, None, 'tensor'), may hold values from -1 to 1
- request_adapter: int32 [16], P('parts'), parts along dimension 0, may hold values from 0 to 31
- cached_lengths: int32 [16], P('parts'), parts along dimension 0, may hold values from 2 to 512, as said below
- rotated_key_cache: bfloat16 [4096, 16, 128], P('tensor', 'parts'), parts along dimension 1, may hold values from -260 to 260
- cached_value_rows: bfloat16 [4096, 16, 128], P('tensor', 'parts'), parts along dimension 1, may hold values from -6 to 6
Outputs:
- states: bfloat16 [2, 16, 8192], P(None, 'parts', 'tensor'), parts along dimension 1
There are 2 independent parts, one for each index of `parts`. A program takes and returns all parts, laid end to end along the dimension named above; an argument that names none is the same for every part. Nothing has to cross between parts.
Inputs may be any that keep to these rules, and one draw needn't show every extreme that they name: `cached_lengths`: at least one request has all 512 positions cached.
All inputs are finite; a program needn't handle non-finite values.
Results may differ from a plain program's by a relative error of at most 0.0062.
Values may be sent and summed in bfloat16 or wider, within the bound.
A program may use at most 128 MiB of HBM per device.

v0:
```python
import jax
import jax.numpy as jnp
from jax import lax
from jax.sharding import PartitionSpec as P

MODEL_WIDTH = 8192
QUERY_HEADS = 64
KEY_VALUE_HEADS = 8
HEAD_DIMENSION = 128
STEPS = 2


theta_base = 500000.0
adapter_scale = 0.5
big_negative = -1e30
eps_norm = 1e-05


def merged(x, axis, combine):
    everything = jax.tree.map(
        lambda part, kind: lax.all_gather(part.astype(kind), axis),
        x,
        (jnp.bfloat16, jnp.bfloat16, jnp.bfloat16),
    )

    def take(k):
        return jax.tree.map(lambda part, own: part[k].astype(own.dtype), everything, x)

    return lax.fori_loop(
        1, lax.axis_size(axis), lambda k, so_far: combine(so_far, take(k)), take(0)
    )


def contract_final_axis(left, right):
    return lax.dot_general(
        left, right, (((1,), (1,)), ((), ())), preferred_element_type=jnp.float32
    )


def rotate_pairs(vectors, offset, positions):
    row_count, col_count = vectors.shape
    paired = vectors.reshape(row_count, col_count // 2, 2)
    pair_index = (offset // 2 + jnp.arange(col_count // 2, dtype=jnp.int32)) % (HEAD_DIMENSION // 2)
    frequency = jnp.power(
        jnp.float32(theta_base), -2.0 * pair_index.astype(jnp.float32) / HEAD_DIMENSION
    )
    angles = positions[:, None] * frequency[None, :]
    cosine = jnp.cos(angles)
    sine_part = jnp.sin(angles)
    even_part = paired[:, :, 0]
    odd_part = paired[:, :, 1]
    turned = jnp.stack(
        [even_part * cosine - odd_part * sine_part, even_part * sine_part + odd_part * cosine],
        axis=2,
    )
    return turned.reshape(row_count, col_count)


def adapter_down_project(normalized_input, adapter_indicator, factor):
    adapter_count, depth_rows, rank_size = factor.shape
    flat_table = jnp.transpose(factor, (1, 0, 2)).reshape(depth_rows, adapter_count * rank_size)
    spread = jnp.dot(normalized_input, flat_table, preferred_element_type=jnp.float32).reshape(
        -1, adapter_count, rank_size
    )
    return jnp.sum(spread * adapter_indicator.astype(jnp.float32)[:, :, None], axis=1)


def adapter_row_select(shrink_low, adapter_indicator, factor):
    spread = (adapter_indicator[:, :, None] * shrink_low[:, None, :]).reshape(
        shrink_low.shape[0], -1
    )
    return jnp.dot(spread, factor.reshape(-1, factor.shape[2]), preferred_element_type=jnp.float32)


def combine_parts(earlier, later):
    peak_one, total_one, summed_one = earlier
    peak_two, total_two, summed_two = later
    peak_both = jnp.maximum(peak_one, peak_two)
    scale_one = jnp.exp(peak_one - peak_both)
    scale_two = jnp.exp(peak_two - peak_both)
    row_count, head_count = peak_one.shape
    head_size = summed_one.shape[1] // head_count
    summed_both = summed_one.reshape(row_count, head_count, head_size) * scale_one[:, :, None]
    summed_both = (
        summed_both + summed_two.reshape(row_count, head_count, head_size) * scale_two[:, :, None]
    )
    return (
        peak_both,
        total_one * scale_one + total_two * scale_two,
        summed_both.reshape(row_count, head_count * head_size),
    )


def local(
    residual_input,
    attention_norm_gain,
    wq,
    wk,
    wv,
    wo,
    query_down_factor,
    query_up_factor,
    value_down_factor,
    value_up_factor,
    request_adapter,
    cached_lengths,
    rotated_key_cache,
    cached_value_rows,
):
    my_index = lax.axis_index("tensor")
    kv_group = my_index % KEY_VALUE_HEADS
    seq_block = my_index // KEY_VALUE_HEADS
    row_count, local_width = residual_input.shape
    ctx_dev = rotated_key_cache.shape[0]
    q_cols = wq.shape[0]
    kv_cols = wk.shape[0]
    per_group = QUERY_HEADS // KEY_VALUE_HEADS
    score_scale = HEAD_DIMENSION ** (-0.5)
    adapter_indicator = (
        request_adapter[:, None] == jnp.arange(query_down_factor.shape[0], dtype=jnp.int32)[None, :]
    ).astype(jnp.bfloat16)
    cache_pos = seq_block * ctx_dev + jnp.arange(ctx_dev, dtype=jnp.int32)
    cache_live = cache_pos[None, :] < cached_lengths[:, None]
    first_block = seq_block == 0
    group_mask = jnp.arange(KEY_VALUE_HEADS, dtype=jnp.int32) == kv_group
    group_float = group_mask.astype(jnp.float32)
    current = residual_input
    outputs = []
    fresh_keys = []
    fresh_values = []
    for step_index in range(STEPS):
        positions = (cached_lengths + step_index).astype(jnp.float32)
        widened = current.astype(jnp.float32)
        squares = lax.psum(jnp.sum(widened * widened, axis=1), "tensor")
        inv_rms = lax.rsqrt(squares / MODEL_WIDTH + eps_norm)
        local_normalized = (
            widened * inv_rms[:, None] * attention_norm_gain.astype(jnp.float32)[None, :]
        ).astype(jnp.bfloat16)
        part_rows = lax.all_gather(local_normalized, "tensor", axis=1, tiled=True)
        query_sum = contract_final_axis(part_rows, wq)
        k_sum = contract_final_axis(part_rows, wk)
        value_sum = contract_final_axis(part_rows, wv)
        query_down_output, value_down_output = lax.psum(
            (
                adapter_down_project(local_normalized, adapter_indicator, query_down_factor),
                adapter_down_project(local_normalized, adapter_indicator, value_down_factor),
            ),
            "tensor",
        )
        query_vector = query_sum + adapter_scale * adapter_row_select(
            query_down_output.astype(jnp.bfloat16), adapter_indicator, query_up_factor
        )
        query_vector = rotate_pairs(query_vector, my_index * q_cols, positions).astype(jnp.bfloat16)
        key_new = rotate_pairs(k_sum, my_index * kv_cols, positions).astype(jnp.bfloat16)
        value_current = (
            value_sum
            + adapter_scale
            * adapter_row_select(
                value_down_output.astype(jnp.bfloat16), adapter_indicator, value_up_factor
            )
        ).astype(jnp.bfloat16)
        full_q, full_k, full_v = (
            lax.all_gather(query_vector, "tensor", axis=1, tiled=True),
            lax.all_gather(key_new, "tensor", axis=1, tiled=True),
            lax.all_gather(value_current, "tensor", axis=1, tiled=True),
        )
        group_q = lax.dynamic_slice_in_dim(
            full_q, kv_group * per_group * HEAD_DIMENSION, per_group * HEAD_DIMENSION, 1
        ).reshape(row_count, per_group, HEAD_DIMENSION)
        fresh_keys.append(
            lax.dynamic_slice_in_dim(full_k, kv_group * HEAD_DIMENSION, HEAD_DIMENSION, 1)
        )
        fresh_values.append(
            lax.dynamic_slice_in_dim(full_v, kv_group * HEAD_DIMENSION, HEAD_DIMENSION, 1)
        )
        fresh_k = jnp.stack(fresh_keys, axis=1)
        fresh_v = jnp.stack(fresh_values, axis=1)
        cached = (
            jnp.einsum(
                "bgd,pbd->bgp", group_q, rotated_key_cache, preferred_element_type=jnp.float32
            )
            * score_scale
        )
        fresh_scores = (
            jnp.einsum("bgd,bsd->bgs", group_q, fresh_k, preferred_element_type=jnp.float32)
            * score_scale
        )
        cached = jnp.where(cache_live[:, None, :], cached, big_negative)
        fresh_scores = jnp.where(first_block, fresh_scores, big_negative)
        local_peak = jnp.maximum(jnp.max(cached, axis=2), jnp.max(fresh_scores, axis=2))
        cache_w = jnp.where(cache_live[:, None, :], jnp.exp(cached - local_peak[:, :, None]), 0.0)
        fresh_w = jnp.where(first_block, jnp.exp(fresh_scores - local_peak[:, :, None]), 0.0)
        local_total = jnp.sum(cache_w, axis=2) + jnp.sum(fresh_w, axis=2)
        weighted = jnp.einsum(
            "bgp,pbd->bgd",
            cache_w.astype(jnp.bfloat16),
            cached_value_rows,
            preferred_element_type=jnp.float32,
        )
        weighted = weighted + jnp.einsum(
            "bgs,bsd->bgd",
            fresh_w.astype(jnp.bfloat16),
            fresh_v,
            preferred_element_type=jnp.float32,
        )
        maxima = jnp.where(group_mask[None, :, None], local_peak[:, None, :], big_negative).reshape(
            row_count, QUERY_HEADS
        )
        totals = (group_float[None, :, None] * local_total[:, None, :]).reshape(
            row_count, QUERY_HEADS
        )
        values_all = (group_float[None, :, None, None] * weighted[:, None, :, :]).reshape(
            row_count, QUERY_HEADS * HEAD_DIMENSION
        )
        peak_all, denominator, summed = merged(
            (maxima, totals, values_all), "tensor", combine_parts
        )
        attention = (
            (summed.reshape(row_count, QUERY_HEADS, HEAD_DIMENSION) / denominator[:, :, None])
            .reshape(row_count, QUERY_HEADS * HEAD_DIMENSION)
            .astype(jnp.bfloat16)
        )
        projected = contract_final_axis(attention, wo)
        current = (widened + projected).astype(jnp.bfloat16)
        outputs.append(current)
    return jnp.stack(outputs, axis=0)


def solution(mesh):
    in_specs = (
        P("parts", "tensor"),
        P("tensor"),
        P("tensor", None),
        P("tensor", None),
        P("tensor", None),
        P("tensor", None),
        P(None, "tensor", None),
        P(None, None, "tensor"),
        P(None, "tensor", None),
        P(None, None, "tensor"),
        P("parts"),
        P("parts"),
        P("tensor", "parts", None),
        P("tensor", "parts", None),
    )
    out_specs = P(None, "parts", "tensor")
    return jax.shard_map(local, mesh=mesh, in_specs=in_specs, out_specs=out_specs, check_vma=False)
```

profile of v0, /device:TPU:0, one launch (start us, length us, event | category | flops | bytes accessed | tf_op | source)
XLA Modules:
  0.0 503.8 jit_solution(13082183029245280062)
XLA Ops:
  9.3 34.9 %psum.42 = f32[8]{0:T(128)S(1)} all-reduce(f32[8]{0:T(128)S(1)} %fusion.69), channel_id=1, replica_groups=mesh['parts'=2,'tensor'=16] {'tensor'}, use_global_device_ids=true, to_apply=%region_1.2 | all-reduce | flops 8 | bytes 64 | tf_op jit(solution)/shard_map/psum | solution.py:134
  45.0 17.5 %all_gather.48 = bf16[8,8192]{1,0:T(8,128)(2,1)S(1)} all-gather(bf16[8,512]{1,0:T(8,128)(2,1)S(1)} %fusion.71), channel_id=1, replica_groups=mesh['parts'=2,'tensor'=16] {'tensor'}, dimensions={1}, use_global_device_ids=true | all-gather | bytes 139264 | tf_op jit(solution)/shard_map/all_gather | solution.py:139
  62.4 2.0 fusion.6
  64.4 2.1 fusion.7
  66.6 32.6 %all-reduce.1 = (bf16[8,32]{1,0:T(8,128)(2,1)S(1)}, bf16[8,32]{1,0:T(8,128)(2,1)}) all-reduce(f32[8,32]{1,0:T(8,128)S(1)} %fusion.6, f32[8,32]{1,0:T(8,128)S(1)} %fusion.7), channel_id=1, replica_groups=mesh['parts'=2,'tensor'=16] {'tensor'}, use_global_device_ids=true, to_apply=%region_3.4 | all-reduce | flops 512 | bytes 3072 | tf_op jit(solution)/shard_map/psum | solution.py:143
  99.2 5.7 %fusion.152 = f32[8,512]{1,0:T(8,128)S(1)} fusion(bf16[8,8192]{1,0:T(8,128)(2,1)S(1)} %all_gather.48, bf16[512,8192]{1,0:T(8,128)(2,1)} %param.20), kind=kOutput, calls=%fused_computation.232 | convolution fusion | flops 67108864 | bytes 8536064 | tf_op jit(solution)/shard_map/dot_general | solution.py:35
  104.9 1.0 fusion.15
  108.6 1.0 copy.212
  109.6 1.2 add_convert_fusion
  111.6 29.2 %all_gather.49 = bf16[8,8192]{0,1:T(8,128)(2,1)} all-gather(bf16[8,512]{0,1:T(8,128)(2,1)S(1)} %bitcast.247), channel_id=1, replica_groups=mesh['parts'=2,'tensor'=16] {'tensor'}, dimensions={1}, use_global_device_ids=true | all-gather | bytes 139264 | tf_op jit(solution)/shard_map/all_gather | solution.py:163
  142.5 1.6 fusion.153
  145.3 17.5 %all-gather = bf16[16,64,8]{1,2,0:T(8,128)(2,1)S(1)} all-gather(bf16[1,64,8]{1,2,0:T(8,128)(2,1)S(1)} %bitcast.256), channel_id=1, replica_groups=mesh['parts'=2,'tensor'=16] {'tensor'}, dimensions={0}, use_global_device_ids=true | all-gather | bytes 17408 | tf_op jit(solution)/shard_map/all_gather | solution.py:164
  164.5 1.0 fusion.149
  166.2 1.3 fusion.27
  167.5 18.8 %all-gather.1 = bf16[16,64,8]{1,2,0:T(8,128)(2,1)S(1)} all-gather(bf16[1,64,8]{1,2,0:T(8,128)(2,1)S(1)} %fusion.27), channel_id=1, replica_groups=mesh['parts'=2,'tensor'=16] {'tensor'}, dimensions={0}, use_global_device_ids=true | all-gather | bytes 17408 | tf_op jit(solution)/shard_map/all_gather | solution.py:165
  190.7 18.9 %all_gather.52 = bf16[16,8,64]{2,1,0:T(8,128)(2,1)} all-gather(bf16[1,8,64]{2,1,0:T(8,128)(2,1)S(1)} %multiply_convert_fusion.3), channel_id=1, replica_groups=mesh['parts'=2,'tensor'=16] {'tensor'}, dimensions={0}, use_global_device_ids=true | all-gather | bytes 17408 | tf_op jit(solution)/shard_map/all_gather | solution.py:21
  209.6 20.4 %all_gather.51 = bf16[16,8,64]{2,1,0:T(8,128)(2,1)} all-gather(bf16[1,8,64]{2,1,0:T(8,128)(2,1)S(1)} %select_convert_fusion.1), channel_id=1, replica_groups=mesh['parts'=2,'tensor'=16] {'tensor'}, dimensions={0}, use_global_device_ids=true | all-gather | bytes 17408 | tf_op jit(solution)/shard_map/all_gather | solution.py:21
  232.3 31.1 %while.38 = (s32[]{:T(128)}, f32[8,64]{1,0:T(8,128)S(1)}, f32[8,64]{1,0:T(8,128)S(1)}, f32[8,8192]{1,0:T(8,128)S(1)}, bf16[16,8,64]{2,1,0:T(8,128)(2,1)}, /*inde...) while((s32[]{:T(128)}, f32[8,64]{1,0:T(8,128)S(1)}, ...), condition=%wide.region_9.10_spmd, body=%wide.region_8.9_spmd.sunk | while | flops 266245 | bytes 682135 | solution.py:29
  233.2 1.2 fusion.185
  235.2 1.2 fusion.185
  237.3 1.2 fusion.185
  239.4 1.2 fusion.185
  241.5 1.2 fusion.185
  243.5 1.2 fusion.185
  245.6 1.2 fusion.185
  247.7 1.2 fusion.185
  249.8 1.2 fusion.185
  251.8 1.2 fusion.185
  253.9 1.2 fusion.185
  256.0 1.2 fusion.185
  258.0 1.2 fusion.185
  260.1 1.2 fusion.185
  262.2 1.2 fusion.185
  263.5 5.8 %fusion.72 = (f32[8]{0:T(128)S(1)}, bf16[8,512]{1,0:T(8,128)(2,1)S(1)}) fusion(bf16[512,8192]{1,0:T(8,128)(2,1)} %param.23, f32[8,8192]{1,0:T(8,128)S(1)} %get-tuple-element.359, f32[8,64]{0,1:T(8,128)S(1)} %copy.184, bf16[8,512]{1,0:T(8,128)(2,1)S(1)} %copy-done.4), kind=kOutput, calls=%fused_computation.107 | convolution fusion | flops 67264504 | bytes 8669216 | tf_op jit(solution)/shard_map/dot_general | solution.py:35
  269.3 30.0 %psum.45 = f32[8]{0:T(128)S(1)} all-reduce(f32[8]{0:T(128)S(1)} %get-tuple-element.431), channel_id=1, replica_groups=mesh['parts'=2,'tensor'=16] {'tensor'}, use_global_device_ids=true, to_apply=%region_11.12 | all-reduce | flops 8 | bytes 64 | tf_op jit(solution)/shard_map/psum | solution.py:134
  299.3 2.0 fusion.8
  301.3 2.0 fusion.9
  303.4 17.5 %all_gather.55 = bf16[8,8192]{1,0:T(8,128)(2,1)S(1)} all-gather(bf16[8,512]{1,0:T(8,128)(2,1)S(1)} %fusion.74), channel_id=1, replica_groups=mesh['parts'=2,'tensor'=16] {'tensor'}, dimensions={1}, use_global_device_ids=true | all-gather | bytes 139264 | tf_op jit(solution)/shard_map/all_gather | solution.py:139
  321.2 1.7 fusion.156
  322.9 5.6 %fusion.155 = f32[8,512]{1,0:T(8,128)S(1)} fusion(bf16[8,8192]{1,0:T(8,128)(2,1)S(1)} %all_gather.55, bf16[512,8192]{1,0:T(8,128)(2,1)} %param.20), kind=kOutput, calls=%fused_computation.235 | convolution fusion | flops 67108864 | bytes 8536064 | tf_op jit(solution)/shard_map/dot_general | solution.py:35
  328.5 32.1 %all-reduce = (bf16[8,32]{1,0:T(8,128)(2,1)S(1)}, bf16[8,32]{1,0:T(8,128)(2,1)S(1)}) all-reduce(f32[8,32]{1,0:T(8,128)S(1)} %fusion.8, f32[8,32]{1,0:T(8,128)S(1)} %fusion.9), channel_id=1, replica_groups=mesh['parts'=2,'tensor'=16] {'tensor'}, use_global_device_ids=true, to_apply=%region_13.14 | all-reduce | flops 512 | bytes 3072 | tf_op jit(solution)/shard_map/psum | solution.py:143
  361.0 17.2 %all-gather.3 = bf16[16,64,8]{1,2,0:T(8,128)(2,1)S(1)} all-gather(bf16[1,64,8]{1,2,0:T(8,128)(2,1)S(1)} %fusion.26), channel_id=1, replica_groups=mesh['parts'=2,'tensor'=16] {'tensor'}, dimensions={0}, use_global_device_ids=true | all-gather | bytes 17408 | tf_op jit(solution)/shard_map/all_gather | solution.py:165
  378.8 19.1 %all-gather.2 = bf16[16,64,8]{1,2,0:T(8,128)(2,1)S(1)} all-gather(bf16[1,64,8]{1,2,0:T(8,128)(2,1)S(1)} %bitcast.257), channel_id=1, replica_groups=mesh['parts'=2,'tensor'=16] {'tensor'}, dimensions={0}, use_global_device_ids=true | all-gather | bytes 17408 | tf_op jit(solution)/shard_map/all_gather | solution.py:164
  399.3 28.5 %all_gather.56 = bf16[8,8192]{0,1:T(8,128)(2,1)S(1)} all-gather(bf16[8,512]{0,1:T(8,128)(2,1)S(1)} %bitcast.248), channel_id=1, replica_groups=mesh['parts'=2,'tensor'=16] {'tensor'}, dimensions={1}, use_global_device_ids=true | all-gather | bytes 139264 | tf_op jit(solution)/shard_map/all_gather | solution.py:163
  430.1 17.6 %all_gather.59 = bf16[16,8,64]{2,1,0:T(8,128)(2,1)S(1)} all-gather(bf16[1,8,64]{2,1,0:T(8,128)(2,1)S(1)} %multiply_convert_fusion.2), channel_id=1, replica_groups=mesh['parts'=2,'tensor'=16] {'tensor'}, dimensions={0}, use_global_device_ids=true | all-gather | bytes 17408 | tf_op jit(solution)/shard_map/all_gather | solution.py:21
  447.8 18.9 %all_gather.58 = bf16[16,8,64]{2,1,0:T(8,128)(2,1)S(1)} all-gather(bf16[1,8,64]{2,1,0:T(8,128)(2,1)S(1)} %select_convert_fusion), channel_id=1, replica_groups=mesh['parts'=2,'tensor'=16] {'tensor'}, dimensions={0}, use_global_device_ids=true | all-gather | bytes 17408 | tf_op jit(solution)/shard_map/all_gather | solution.py:21
  466.7 2.1 all-gather.9.cloned.1.call-done
  469.7 20.9 %while.39 = (s32[]{:T(128)}, f32[8,64]{1,0:T(8,128)S(1)}, f32[8,64]{1,0:T(8,128)S(1)}, f32[8,8192]{1,0:T(8,128)S(1)}, bf16[16,8,64]{2,1,0:T(8,128)(2,1)S(1)}, /*...) while((s32[]{:T(128)}, f32[8,64]{1,0:T(8,128)S(1)}, ...), condition=%wide.region_21.22_spmd, body=%wide.region_20.21_spmd.sunk | while | flops 266245 | bytes 682135 | solution.py:29
  469.9 1.2 fusion.187
  471.3 1.2 fusion.187
  472.7 1.2 fusion.187
  474.1 1.2 fusion.187
  475.5 1.2 fusion.187
  476.9 1.2 fusion.187
  478.3 1.2 fusion.187
  479.7 1.2 fusion.187
  481.1 1.2 fusion.187
  482.5 1.2 fusion.187
  483.9 1.2 fusion.187
  485.3 1.2 fusion.187
  486.7 1.2 fusion.187
  488.1 1.2 fusion.187
  489.5 1.2 fusion.187
  490.7 5.6 %fusion.18 = bf16[1,8,512]{2,1,0:T(8,128)(2,1)S(1)} fusion(bf16[512,8192]{1,0:T(8,128)(2,1)} %param.23, f32[8,8192]{1,0:T(8,128)S(1)} %get-tuple-element.361, f32[8,64]{0,1:T(8,128)S(1)} %copy.204, bf16[8,512]{1,0:T(8,128)(2,1)S(1)} %get-tuple-element.432), kind=kOutput, calls=%fused_computation.42 | convolution fusion | flops 67252224 | bytes 8669184 | tf_op jit(solution)/shard_map/dot_general | solution.py:35
  (239 shorter events, 41.1 us)
Async XLA Ops:
  6.5 98.3 %copy-start = (bf16[32,32,512]{2,1,0:T(8,128)(2,1)S(1)}, bf16[32,32,512]{2,1,0:T(8,128)(2,1)}, u32[]{:S(2)}) copy-start(bf16[32,32,512]{2,1,0:T(8,128)(2,1)} %param.25) | copy-start | bytes 3145732
  6.5 224.8 %all-gather.7.cloned.1.call-start = ((), (), s32[]{:S(2)}) async-start(), calls=%async_computation | async-start | bytes 2228224 | tf_op jit(solution)/shard_map/all_gather | solution.py:21
  7.1 137.0 %copy-start.8 = (f32[256]{0:T(256)}, f32[256]{0:T(256)S(1)}, u32[]{:S(2)}) copy-start(f32[256]{0:T(256)S(1)} %fusion.129) | copy-start | bytes 3076
  7.8 58.7 %copy-start.5 = (f32[8,32]{0,1:T(8,128)}, f32[8,32]{0,1:T(8,128)S(1)}, u32[]{:S(2)}) copy-start(f32[8,32]{0,1:T(8,128)S(1)} %get-tuple-element.428) | copy-start | bytes 3076
  7.8 97.1 %copy-start.6 = (bf16[8,32]{0,1:T(8,128)(2,1)}, bf16[8,32]{0,1:T(8,128)(2,1)S(1)}, u32[]{:S(2)}) copy-start(bf16[8,32]{0,1:T(8,128)(2,1)S(1)} %get-tuple-element.427) | copy-start | bytes 1540
  64.4 100.1 %copy-start.2 = (bf16[256,8,128]{2,1,0:T(8,128)(2,1)S(1)}, bf16[256,8,128]{2,1,0:T(8,128)(2,1)}, u32[]{:S(2)}) copy-start(bf16[256,8,128]{2,1,0:T(8,128)(2,1)} %param.30) | copy-start | bytes 1572868
  66.5 99.3 %copy-start.1 = (bf16[64,8192]{1,0:T(8,128)(2,1)S(1)}, bf16[64,8192]{1,0:T(8,128)(2,1)}, u32[]{:S(2)}) copy-start(bf16[64,8192]{1,0:T(8,128)(2,1)} %param.22) | copy-start | bytes 3145732
  99.2 87.3 %copy-start.3 = (bf16[256,8,128]{2,1,0:T(8,128)(2,1)S(1)}, bf16[256,8,128]{2,1,0:T(8,128)(2,1)}, u32[]{:S(2)}) copy-start(bf16[256,8,128]{2,1,0:T(8,128)(2,1)} %param.31) | copy-start | bytes 1572868
  104.9 158.6 %copy-start.4 = (bf16[8,512]{1,0:T(8,128)(2,1)S(1)}, bf16[8,512]{1,0:T(8,128)(2,1)}, u32[]{:S(2)}) copy-start(bf16[8,512]{1,0:T(8,128)(2,1)} %param.18) | copy-start | bytes 24580
  110.9 0.6 copy-start.14
  142.5 23.1 %copy-start.15 = (f32[32]{0:T(128)}, f32[32]{0:T(128)S(1)}, u32[]{:S(2)}) copy-start(f32[32]{0:T(128)S(1)} %fusion.134) | copy-start | bytes 388
  188.2 280.6 %all-gather.9.cloned.1.call-start = ((), (), s32[]{:S(2)}) async-start(), calls=%async_computation.1 | async-start | bytes 2228224 | tf_op jit(solution)/shard_map/all_gather | solution.py:21
  190.1 73.4 %copy-start.11 = (pred[64]{0:T(512)(128)(4,1)}, pred[64]{0:T(512)(128)(4,1)S(1)}, u32[]{:S(2)}) copy-start(pred[64]{0:T(512)(128)(4,1)S(1)} %broadcast_in_dim.140) | copy-start | bytes 196
  269.2 91.4 %copy-start.7 = (bf16[8,32]{0,1:T(8,128)(2,1)S(1)}, bf16[8,32]{0,1:T(8,128)(2,1)}, u32[]{:S(2)}) copy-start(bf16[8,32]{0,1:T(8,128)(2,1)} %copy-done.6) | copy-start | bytes 1540
  269.2 91.4 %copy-start.17 = (bf16[32,32,64]{2,1,0:T(8,128)(2,1)S(1)}, bf16[32,32,64]{2,1,0:T(8,128)(2,1)}, u32[]{:S(2)}) copy-start(bf16[32,32,64]{2,1,0:T(8,128)(2,1)} %param.27) | copy-start | bytes 393220
  269.3 109.2 %copy-start.13 = (f32[8]{0:T(128)S(1)}, f32[8]{0:T(128)}, u32[]{:S(2)}) copy-start(f32[8]{0:T(128)} %get-tuple-element.425) | copy-start | bytes 100
  269.3 109.2 %copy-start.16 = (f32[32]{0:T(128)S(1)}, f32[32]{0:T(128)}, u32[]{:S(2)}) copy-start(f32[32]{0:T(128)} %copy-done.15) | copy-start | bytes 388
  269.3 129.7 %copy-start.9 = (f32[256]{0:T(256)S(1)}, f32[256]{0:T(256)}, u32[]{:S(2)}) copy-start(f32[256]{0:T(256)} %copy-done.8) | copy-start | bytes 3076
  321.2 107.1 %copy-start.10 = (bf16[8,1,128]{2,1,0:T(2,128)(2,1)S(1)}, bf16[8,1,128]{2,1,0:T(2,128)(2,1)}, u32[]{:S(2)}) copy-start(bf16[8,1,128]{2,1,0:T(2,128)(2,1)} %copy.197) | copy-start | bytes 6148
  322.9 124.9 %copy-start.12 = (pred[64]{0:T(512)(128)(4,1)S(1)}, pred[64]{0:T(512)(128)(4,1)}, u32[]{:S(2)}) copy-start(pred[64]{0:T(512)(128)(4,1)} %copy-done.11) | copy-start | bytes 196
Sparse Core Ops, SparseCore 0:
  188.3 38.8 all-gather.6
  429.8 38.9 all-gather.8
where the time goes:
time: 506 us; the launch traced here: 504 us
  blocking collectives  371 us (73%)
  other arithmetic  58.5 us (12%)
  matrix products  41 us (8%)
  local copies, waits for them, and re-layouts  16.5 us (3%)
  between operations  13.9 us (3%)
    all_gather x4, blocking collectives, merged(): lax.all_gather(part.astype(kind), axis)  75.9 us
    psum x2, blocking collectives, local(): squares = lax.psum(jnp.sum(widened * widened, axis=1), 'tensor')  64.8 us
    psum x2, blocking collectives, local(): lax.psum((adapter_down_project(local_normalized, adapter_indicator, query...  64.7 us
    all_gather x2, blocking collectives, local(): lax.all_gather(query_vector, 'tensor', axis=1, tiled=True)  57.7 us
    all_gather x2, blocking collectives, local(): lax.all_gather(key_new, 'tensor', axis=1, tiled=True)  36.7 us
    all_gather x2, blocking collectives, local(): lax.all_gather(value_current, 'tensor', axis=1, tiled=True)  36 us
    add x30, other arithmetic, combine_parts(): summed_both + summed_two.reshape(row_count, head_count, head_size) * scal...  35.3 us
    all_gather x2, blocking collectives, local(): part_rows = lax.all_gather(local_normalized, 'tensor', axis=1, tiled=True)  34.9 us
  transfers between devices with their start and end apart: 2, of which 1 were waited for; matrix products, arithmetic and copies ran while one was open for 1% of the time, Pallas kernels for 0%

commit v1 on v0

--- a/solution.py
+++ b/solution.py
@@ -1,6 +1,11 @@
+import functools
+import math
+
 import jax
 import jax.numpy as jnp
 from jax import lax
+from jax.experimental import pallas as pl
+from jax.experimental.pallas import tpu as pltpu
 from jax.sharding import PartitionSpec as P
 
 MODEL_WIDTH = 8192
@@ -226,7 +231,532 @@
     return jnp.stack(outputs, axis=0)
 
 
+def fused_kernel(
+    n,
+    ctx_dev,
+    current_ref,
+    gain_ref,
+    adapter_ref,
+    length_ref,
+    wq_hbm,
+    wk_hbm,
+    wv_hbm,
+    wo_hbm,
+    qd_hbm,
+    qu_hbm,
+    vd_hbm,
+    vu_hbm,
+    kc_hbm,
+    vc_hbm,
+    out_ref,
+    w_s,
+    wo_s,
+    qd_s,
+    vd_s,
+    qu_s,
+    vu_s,
+    k_s,
+    v_s,
+    dq_s,
+    dv_s,
+    uq_s,
+    uv_s,
+    xg,
+    sg,
+    qg,
+    og,
+    xsend,
+    ssend,
+    qsend,
+    osend,
+    norm_s,
+    attn_s,
+    gain_s,
+    load_sem,
+    x_send_sem,
+    x_recv_sem,
+    s_send_sem,
+    s_recv_sem,
+    q_send_sem,
+    q_recv_sem,
+    o_send_sem,
+    o_recv_sem,
+):
+    f32, bf16 = jnp.float32, jnp.bfloat16
+    hd, groups = HEAD_DIMENSION, KEY_VALUE_HEADS
+    rows, width = current_ref.shape
+    q_cols, kv_cols = wq_hbm.shape[0], wk_hbm.shape[0]
+    chunks = width // hd
+    heads_here = q_cols // hd
+    per_group = QUERY_HEADS // groups
+    blocks = n // groups
+    cached_rows = ctx_dev * rows
+    rank = qd_hbm.shape[1]
+    me = lax.axis_index("tensor")
+
+    loads = []
+
+    def load(src, dst):
+        copy = pltpu.make_async_copy(src, dst, load_sem.at[len(loads)])
+        copy.start()
+        loads.append(copy)
+        return copy
+
+    small = [
+        load(qd_hbm, qd_s),
+        load(vd_hbm, vd_s),
+    ]
+    pieces = 4
+    step_cols = MODEL_WIDTH // pieces
+    weights = []
+    for piece in range(pieces):
+        cols = pl.ds(piece * step_cols, step_cols)
+        weights.append(
+            [
+                load(wq_hbm.at[:, cols], w_s.at[pl.ds(0, q_cols), cols]),
+                load(wk_hbm.at[:, cols], w_s.at[pl.ds(q_cols, kv_cols), cols]),
+                load(wv_hbm.at[:, cols], w_s.at[pl.ds(q_cols + kv_cols, kv_cols), cols]),
+            ]
+        )
+    ups = [load(qu_hbm, qu_s), load(vu_hbm, vu_s)]
+    caches = [
+        load(kc_hbm, k_s.at[pl.ds(0, cached_rows)]),
+        load(vc_hbm, v_s.at[pl.ds(0, cached_rows)]),
+    ]
+    out_weights = []
+    for piece in range(pieces):
+        cols = pl.ds(piece * step_cols, step_cols)
+        out_weights.append(load(wo_hbm.at[:, cols], wo_s.at[:, cols]))
+
+    barrier = pltpu.get_barrier_semaphore()
+
+    def greet(k, carry):
+        pl.semaphore_signal(
+            barrier,
+            inc=1,
+            device_id={"tensor": lax.rem(me + k, n)},
+            device_id_type=pl.DeviceIdType.MESH,
+        )
+        return carry
+
+    lax.fori_loop(1, n, greet, 0)
+
+    def remote(src, dst, send_sem, recv_sem, target):
+        return pltpu.make_async_remote_copy(
+            src_ref=src,
+            dst_ref=dst,
+            send_sem=send_sem,
+            recv_sem=recv_sem,
+            device_id={"tensor": target},
+            device_id_type=pl.DeviceIdType.MESH,
+        )
+
+    def for_others(body):
+        def step(k, carry):
+            body(lax.rem(me + k, n))
+            return carry
+
+        lax.fori_loop(1, n, step, 0)
+
+    def x_copy(t, slot, target):
+        size = xsend.shape[1] if t == 0 else chunks * rows
+        return remote(
+            xsend.at[t, pl.ds(0, size)],
+            xg.at[t, slot, pl.ds(0, size)],
+            x_send_sem.at[t, target],
+            x_recv_sem.at[t, slot],
+            target,
+        )
+
+    def s_copy(t, slot, target):
+        return remote(
+            ssend.at[t], sg.at[t, slot], s_send_sem.at[t, target], s_recv_sem.at[t, slot], target
+        )
+
+    def o_copy(t, slot, target):
+        return remote(
+            osend.at[t], og.at[t, slot], o_send_sem.at[t, target], o_recv_sem.at[t, slot], target
+        )
+
+    def q_copy(t, slot, block, target):
+        return remote(
+            qsend.at[t], qg.at[t, slot], q_send_sem.at[t, block], q_recv_sem.at[t, slot], target
+        )
+
+    lane = lax.broadcasted_iota(jnp.int32, (rows, hd), 1)
+    row = lax.broadcasted_iota(jnp.int32, (rows, hd), 0)
+    gains = gain_ref[...]
+    row16 = lax.broadcasted_iota(jnp.int32, (16, hd), 0)
+
+    def split_chunks(x):
+        return [x[:, c * hd : (c + 1) * hd] for c in range(x.shape[1] // hd)]
+
+    current = current_ref[...].astype(f32)
+    gain16 = jnp.zeros((16, hd), f32)
+    for c, piece in enumerate(split_chunks(gains)):
+        gain16 = jnp.where(row16 == c, piece[0:1, :], gain16)
+
+    def send_state(t):
+        parts = split_chunks(current) + ([gain16] if t == 0 else [])
+        message = jnp.concatenate(parts, axis=0).astype(bf16)
+        xsend[t, pl.ds(0, message.shape[0])] = message
+        xg[t, me, pl.ds(0, message.shape[0])] = message
+        if t == 0:
+            pl.semaphore_wait(barrier, n - 1)
+        for_others(lambda target: x_copy(t, me, target).start())
+
+    send_state(0)
+
+    lengths = jnp.zeros((rows, hd), jnp.int32)
+    for r in range(rows):
+        lengths = jnp.where(row == r, length_ref[r], lengths)
+    lane_even = lax.rem(lane, 2) == 0
+
+    def angle_tables(pair, positions):
+        frequency = jnp.exp(pair.astype(f32) * jnp.float32(-2.0 * math.log(theta_base) / hd))
+        angles = positions * frequency
+        sine = jnp.sin(angles)
+        return jnp.cos(angles), jnp.where(lane_even, -sine, sine)
+
+    fresh_pair = lax.rem(me, 2) * (kv_cols // 2) + lax.rem(lane, kv_cols) // 2
+    is_key = lane < kv_cols
+    tables = []
+    for t in range(STEPS):
+        positions = (lengths + t).astype(f32)
+        q_cos, q_sin = angle_tables(lane // 2, positions)
+        k_cos, k_sin = angle_tables(fresh_pair, positions)
+        tables.append(
+            (q_cos, q_sin, jnp.where(is_key, k_cos, 1.0), jnp.where(is_key, k_sin, 0.0))
+        )
+
+    def rotate(x, cosine, sine):
+        swapped = jnp.where(lane_even, pltpu.roll(x, hd - 1, 1), pltpu.roll(x, 1, 1))
+        return x * cosine + swapped * sine
+
+    extra = k_s.shape[0] - cached_rows
+    k_s[pl.ds(cached_rows, extra)] = jnp.zeros((extra, hd), bf16)
+    v_s[pl.ds(cached_rows, extra)] = jnp.zeros((extra, hd), bf16)
+
+    column = lax.broadcasted_iota(jnp.int32, (rows, cached_rows + extra), 1)
+    wide_row = lax.broadcasted_iota(jnp.int32, (rows, cached_rows + extra), 0)
+    seq_block = me // groups
+    wide_length = jnp.zeros((rows, cached_rows + extra), jnp.int32)
+    for r in range(rows):
+        wide_length = jnp.where(wide_row == r, length_ref[r], wide_length)
+    own_cached = (
+        (column < cached_rows)
+        & (lax.rem(column, rows) == wide_row)
+        & (seq_block * ctx_dev + column // rows < wide_length)
+    )
+    fresh_column = column - cached_rows
+    fresh_row = (fresh_column >= 0) & (lax.rem(column, 16) == wide_row) & (seq_block == 0)
+
+    for copy in small:
+        copy.wait()
+    for r in range(rows):
+        adapter = adapter_ref[r]
+        dq_s[pl.ds(r * rank, rank)] = qd_s[adapter]
+        dv_s[pl.ds(r * rank, rank)] = vd_s[adapter]
+
+    spread_column = lax.broadcasted_iota(jnp.int32, (rows, rows * rank), 1)
+    spread_row = lax.broadcasted_iota(jnp.int32, (rows, rows * rank), 0)
+    own_block = spread_column // rank == spread_row
+    even_block = lax.rem(lane // rank, 2) == 0
+
+    def contract(left, right):
+        return lax.dot_general(
+            left, right, (((1,), (1,)), ((), ())), preferred_element_type=f32
+        )
+
+    def fold(x):
+        x = jnp.where(own_block, x, 0.0)
+        parts = split_chunks(x)
+        total = parts[0]
+        for part in parts[1:]:
+            total = total + part
+        shift = hd // 2
+        while shift >= rank:
+            total = total + pltpu.roll(total, shift, 1)
+            shift //= 2
+        return total
+
+    def send_shrink(t):
+        scaled = (current * gains).astype(bf16)
+        both = jnp.where(
+            even_block, fold(contract(scaled, dq_s[...])), fold(contract(scaled, dv_s[...]))
+        )
+        ssend[t] = both
+        sg[t, me] = both
+        for_others(lambda target: s_copy(t, me, target).start())
+
+    send_shrink(0)
+
+    for t in range(STEPS):
+        for_others(lambda source: x_copy(t, source, source).wait_recv())
+        squares = jnp.zeros((rows, hd), f32)
+        for d in range(n):
+            block = xg[t, d, pl.ds(0, chunks * rows)].astype(f32)
+            for c in range(chunks):
+                part = block[c * rows : (c + 1) * rows]
+                squares = squares + part * part
+            if t == 0:
+                gain_block = xg[0, d, pl.ds(chunks * rows, 16)].astype(f32)
+                gain_s[pl.ds(d * chunks, chunks)] = gain_block[0:chunks]
+        total = jnp.sum(squares, axis=1, keepdims=True)
+        inv_rms = lax.rsqrt(total / MODEL_WIDTH + eps_norm)
+        for d in range(n):
+            block = xg[t, d, pl.ds(0, chunks * rows)].astype(f32)
+            for c in range(chunks):
+                at = d * chunks + c
+                part = block[c * rows : (c + 1) * rows]
+                normed = part * inv_rms * gain_s[pl.ds(at, 1)]
+                norm_s[:, pl.ds(at * hd, hd)] = normed.astype(bf16)
+        products = jnp.zeros((rows, q_cols + 2 * kv_cols), f32)
+        for piece in range(pieces):
+            cols = pl.ds(piece * step_cols, step_cols)
+            if t == 0:
+                for copy in weights[piece]:
+                    copy.wait()
+            products = products + contract(norm_s[:, cols], w_s[:, cols])
+        if t == 0:
+            for copy in ups:
+                copy.wait()
+            for r in range(rows):
+                adapter = adapter_ref[r]
+                uq_s[pl.ds(r * rank, rank)] = qu_s[adapter]
+                uv_s[pl.ds(r * rank, rank)] = vu_s[adapter]
+        for_others(lambda source: s_copy(t, source, source).wait_recv())
+        shrink = sg[t, 0]
+        for d in range(1, n):
+            shrink = shrink + sg[t, d]
+        shrink = shrink * inv_rms
+        turned = pltpu.roll(shrink, rank, 1)
+
+        def spread(x):
+            x = jnp.concatenate([x] * (rows * rank // hd), axis=1)
+            return jnp.where(own_block, x, 0.0).astype(bf16)
+
+        q_low = spread(jnp.where(even_block, shrink, turned))
+        v_low = spread(jnp.where(even_block, turned, shrink))
+        q_up = jnp.dot(q_low, uq_s[...], preferred_element_type=f32)
+        v_up = jnp.dot(v_low, uv_s[...], preferred_element_type=f32)
+        query = products[:, :q_cols] + adapter_scale * q_up
+        fresh = products[:, q_cols:] + adapter_scale * jnp.concatenate(
+            [jnp.zeros((rows, kv_cols), f32), v_up], axis=1
+        )
+        q_cos, q_sin, k_cos, k_sin = tables[t]
+        parts = [rotate(part, q_cos, q_sin) for part in split_chunks(query)]
+        parts.append(rotate(fresh, k_cos, k_sin))
+        parts.append(jnp.zeros((rows, hd), f32))
+        message = jnp.concatenate(parts, axis=0).astype(bf16)
+        qsend[t] = message
+        side = lax.rem(me, 2)
+        for block in range(blocks):
+            target = me // 2 + block * groups
+
+            @pl.when(target == me)
+            def _():
+                qg[t, side] = message
+
+            @pl.when(target != me)
+            def _():
+                q_copy(t, side, block, target).start()
+
+        if t == 0:
+            for copy in caches:
+                copy.wait()
+        for half in range(2):
+            source = 2 * lax.rem(me, groups) + half
+
+            @pl.when(source != me)
+            def _():
+                q_copy(t, half, 0, source).wait_recv()
+
+        first = qg[t, 0].astype(f32)
+        second = qg[t, 1].astype(f32)
+        q_rows = heads_here * rows
+        queries = jnp.concatenate([first[:q_rows], second[:q_rows]], axis=0).astype(bf16)
+        first_kv = first[q_rows : q_rows + rows]
+        second_kv = second[q_rows : q_rows + rows]
+        key_new = jnp.where(is_key, first_kv, pltpu.roll(second_kv, kv_cols, 1))
+        value_new = jnp.where(is_key, pltpu.roll(first_kv, kv_cols, 1), second_kv)
+        blank = jnp.zeros((16 - rows, hd), f32)
+        k_s[pl.ds(cached_rows + 16 * t, 16)] = jnp.concatenate([key_new, blank], 0).astype(bf16)
+        v_s[pl.ds(cached_rows + 16 * t, 16)] = jnp.concatenate([value_new, blank], 0).astype(bf16)
+        scores = contract(queries, k_s[...]) * (HEAD_DIMENSION ** (-0.5))
+        scores = scores.reshape(per_group, rows, cached_rows + extra)
+        live = (own_cached | (fresh_row & (fresh_column < 16 * (t + 1))))[None]
+        scores = jnp.where(live, scores, big_negative)
+        peak = jnp.max(scores, axis=2, keepdims=True)
+        weight = jnp.where(live, jnp.exp(scores - peak), 0.0)
+        mass = jnp.sum(weight, axis=2, keepdims=True)
+        weight = weight.reshape(per_group * rows, cached_rows + extra).astype(bf16)
+        summed = jnp.dot(weight, v_s[...], preferred_element_type=f32)
+        summed = summed.reshape(per_group, rows, hd)
+        some = mass > 0.0
+        safe = jnp.where(some, mass, 1.0)
+        partial = summed / safe
+        level = jnp.where(some, peak + jnp.log(safe), big_negative)
+        levels = jnp.zeros((rows, hd), f32)
+        for h in range(per_group):
+            levels = jnp.where(lane == h, level[h], levels)
+        high = levels.astype(bf16).astype(f32)
+        middle = (levels - high).astype(bf16).astype(f32)
+        low = levels - high - middle
+        packed = high + pltpu.roll(middle, per_group, 1) + pltpu.roll(low, 2 * per_group, 1)
+        message = jnp.concatenate(
+            [partial.reshape(per_group * rows, hd), packed, jnp.zeros((16 - rows, hd), f32)], axis=0
+        ).astype(bf16)
+        osend[t] = message
+        og[t, me] = message
+        for_others(lambda target: o_copy(t, me, target).start())
+        for_others(lambda source: o_copy(t, source, source).wait_recv())
+        for g in range(groups):
+            found = []
+            for b in range(blocks):
+                entry = og[t, b * groups + g].astype(f32)
+                packed = entry[per_group * rows : per_group * rows + rows]
+                level = (
+                    packed
+                    + pltpu.roll(packed, hd - per_group, 1)
+                    + pltpu.roll(packed, hd - 2 * per_group, 1)
+                )
+                found.append((level, entry))
+            top = found[0][0]
+            for level, _ in found[1:]:
+                top = jnp.maximum(top, level)
+            shares = [jnp.exp(level - top) for level, _ in found]
+            whole = shares[0]
+            for share in shares[1:]:
+                whole = whole + share
+            for h in range(per_group):
+                value = jnp.zeros((rows, hd), f32)
+                for share, (_, entry) in zip(shares, found):
+                    part = (share / whole)[:, h : h + 1]
+                    value = value + part * entry[h * rows : (h + 1) * rows]
+                attn_s[:, pl.ds((g * per_group + h) * hd, hd)] = value.astype(bf16)
+        projected = jnp.zeros((rows, width), f32)
+        for piece in range(pieces):
+            cols = pl.ds(piece * step_cols, step_cols)
+            if t == 0:
+                out_weights[piece].wait()
+            projected = projected + contract(attn_s[:, cols], wo_s[:, cols])
+        rounded = (current + projected).astype(bf16)
+        out_ref[t] = rounded
+        current = rounded.astype(f32)
+        if t + 1 < STEPS:
+            send_state(t + 1)
+            send_shrink(t + 1)
+
+    for t in range(STEPS):
+        for_others(lambda target: x_copy(t, me, target).wait_send())
+        for_others(lambda target: s_copy(t, me, target).wait_send())
+        for_others(lambda target: o_copy(t, me, target).wait_send())
+        for block in range(blocks):
+            target = me // 2 + block * groups
+
+            @pl.when(target != me)
+            def _():
+                q_copy(t, 0, block, target).wait_send()
+
+
+def fused(
+    n,
+    residual_input,
+    attention_norm_gain,
+    wq,
+    wk,
+    wv,
+    wo,
+    query_down_factor,
+    query_up_factor,
+    value_down_factor,
+    value_up_factor,
+    request_adapter,
+    cached_lengths,
+    rotated_key_cache,
+    cached_value_rows,
+):
+    rows, width = residual_input.shape
+    ctx_dev = rotated_key_cache.shape[0]
+    q_cols, kv_cols = wq.shape[0], wk.shape[0]
+    adapters, _, rank = query_down_factor.shape
+    hd = HEAD_DIMENSION
+    chunks = width // hd
+    per_group = QUERY_HEADS // KEY_VALUE_HEADS
+    blocks = n // KEY_VALUE_HEADS
+    kv_rows = ctx_dev * rows + 128
+    x_rows = chunks * rows + 16
+    q_rows = (q_cols // hd + 2) * rows
+    o_rows = per_group * rows + 16
+    bf16, f32 = jnp.bfloat16, jnp.float32
+    dma = pltpu.SemaphoreType.DMA
+    any_spec = pl.BlockSpec(memory_space=pl.ANY)
+    vmem = pl.BlockSpec(memory_space=pltpu.VMEM)
+    smem = pl.BlockSpec(memory_space=pltpu.SMEM)
+    return pl.pallas_call(
+        functools.partial(fused_kernel, n, ctx_dev),
+        out_shape=jax.ShapeDtypeStruct((STEPS, rows, width), bf16),
+        in_specs=[vmem, vmem, smem, smem] + [any_spec] * 10,
+        out_specs=vmem,
+        scratch_shapes=[
+            pltpu.VMEM((q_cols + 2 * kv_cols, MODEL_WIDTH), bf16),
+            pltpu.VMEM((width, MODEL_WIDTH), bf16),
+            pltpu.VMEM((adapters, rank, width), bf16),
+            pltpu.VMEM((adapters, rank, width), bf16),
+            pltpu.VMEM((adapters, rank, q_cols), bf16),
+            pltpu.VMEM((adapters, rank, kv_cols), bf16),
+            pltpu.VMEM((kv_rows, hd), bf16),
+            pltpu.VMEM((kv_rows, hd), bf16),
+            pltpu.VMEM((rows * rank, width), bf16),
+            pltpu.VMEM((rows * rank, width), bf16),
+            pltpu.VMEM((rows * rank, q_cols), bf16),
+            pltpu.VMEM((rows * rank, kv_cols), bf16),
+            pltpu.VMEM((STEPS, n, x_rows, hd), bf16),
+            pltpu.VMEM((STEPS, n, rows, hd), f32),
+            pltpu.VMEM((STEPS, 2, q_rows, hd), bf16),
+            pltpu.VMEM((STEPS, n, o_rows, hd), bf16),
+            pltpu.VMEM((STEPS, x_rows, hd), bf16),
+            pltpu.VMEM((STEPS, rows, hd), f32),
+            pltpu.VMEM((STEPS, q_rows, hd), bf16),
+            pltpu.VMEM((STEPS, o_rows, hd), bf16),
+            pltpu.VMEM((rows, MODEL_WIDTH), bf16),
+            pltpu.VMEM((rows, QUERY_HEADS * hd), bf16),
+            pltpu.VMEM((MODEL_WIDTH // hd, hd), f32),
+            dma((24,)),
+            dma((STEPS, n)),
+            dma((STEPS, n)),
+            dma((STEPS, n)),
+            dma((STEPS, n)),
+            dma((STEPS, blocks)),
+            dma((STEPS, 2)),
+            dma((STEPS, n)),
+            dma((STEPS, n)),
+        ],
+        compiler_params=pltpu.CompilerParams(
+            collective_id=0, has_side_effects=True, vmem_limit_bytes=56 * 1024 * 1024
+        ),
+    )(
+        residual_input,
+        jnp.broadcast_to(attention_norm_gain.astype(f32)[None, :], (rows, width)),
+        request_adapter,
+        cached_lengths,
+        wq,
+        wk,
+        wv,
+        wo,
+        jnp.swapaxes(query_down_factor, 1, 2),
+        query_up_factor,
+        jnp.swapaxes(value_down_factor, 1, 2),
+        value_up_factor,
+        rotated_key_cache.reshape(ctx_dev * rows, hd),
+        cached_value_rows.reshape(ctx_dev * rows, hd),
+    )
+
+
 def solution(mesh):
+    n = mesh.shape["tensor"]
+    body = functools.partial(fused, n) if n == 2 * KEY_VALUE_HEADS else local
     in_specs = (
         P("parts", "tensor"),
         P("tensor"),
@@ -244,4 +774,4 @@
         P("tensor", "parts", None),
     )
     out_specs = P(None, "parts", "tensor")
-    return jax.shard_map(local, mesh=mesh, in_specs=in_specs, out_specs=out_specs, check_vma=False)
+    return jax.shard_map(body, mesh=mesh, in_specs=in_specs, out_specs=out_specs, check_vma=False)

time: 506 us -> 61.6 us (0.12)
  blocking collectives: 371 us -> 0 us
  other arithmetic: 58.5 us -> 0 us
  Pallas kernels: 0 us -> 58.1 us
  matrix products: 41 us -> 0 us
  local copies, waits for them, and re-layouts: 16.5 us -> 2.61 us
  between operations: 13.9 us -> 0.01 us
    all_gather x12 -> x0, blocking collectives: 241 us -> none  [the longest x4 75.9 us: merged(): lax.all_gather(part.astype(kind), axis)]
    psum x4 -> x0, blocking collectives: 130 us -> none  [the longest x2 64.8 us: local(): squares = lax.psum(jnp.sum(widened * widened, axis=1), 'tensor')]
    pallas_call x0 -> x1, Pallas kernels: none -> 58.1 us  [fused(): pl.pallas_call(functools.partial(fused_kernel, n, ctx_dev), out_shape=jax...]
    add x62 -> x0, other arithmetic: 46 us -> none  [the longest x30 35.3 us: combine_parts(): summed_both + summed_two.reshape(row_count, head_count, head_size) * scal...]
    dot_general x23 -> x0, matrix products: 41 us -> none  [the longest x8 26.8 us: contract_final_axis(): lax.dot_general(left, right, (((1,), (1,)), ((), ())), preferred_element_...]
    convert_element_type x17 -> x0, other arithmetic: 8.06 us -> none  [the longest x6 3.2 us: take(): part[k].astype(own.dtype)]
  transfers between devices with their start and end apart: 2 -> 0, of which waited for: 1 -> 0; matrix products, arithmetic and copies ran while one was open for 1% -> 0% of each run, Pallas kernels for 0% -> 0%
where the time goes in v1:
time: 61.6 us; the launch traced here: 60.8 us
  Pallas kernels  58.1 us (94%)
  local copies, waits for them, and re-layouts  2.61 us (4%)
    pallas_call x1, Pallas kernels, fused(): pl.pallas_call(functools.partial(fused_kernel, n, ctx_dev), out_shape=jax...  58.1 us
    unnamed x1, local copies, waits for them, and re-layouts  1.32 us
    broadcast_in_dim x1, local copies, waits for them, and re-layouts, fused(): jnp.broadcast_to(attention_norm_gain.astype(f32)[None, :], (rows, width))  1.29 us

profile of v1, /device:TPU:0, one launch (start us, length us, event | category | flops | bytes accessed | tf_op | source)
XLA Modules:
  0.0 60.8 jit_solution(9979339588266473611)
XLA Ops:
  0.0 1.3 %broadcast_in_dim.2.gain_ref = f32[8,512]{1,0:T(8,128)} broadcast(bf16[512]{0:T(512)(128)(2,1)} %param.15), dimensions={1} | broadcast | bytes 17408 | tf_op jit(solution)/shard_map/broadcast_in_dim | solution.py:741
  1.3 58.1 %shard_map.136 = bf16[2,8,512]{2,1,0:T(8,128)(2,1)} custom-call(bf16[8,512]{1,0:T(8,128)(2,1)} %current_ref.1, f32[8,512]{1,0:T(8,128)} %broadcast_in_dim.2.gain_ref, s32[8]{0:T(128)} %adapter_ref.1, s32[8]{0:T(128)} %length_ref.1, bf16[512,8192]{1,0:T(8,128)(2,1)} %wq_hbm.1, bf16[64,8192]{1,0:T(8,128)(2,1)} %wk_hbm.1, bf16[64,8192]{1,0:T(8,128)(2,1)} %wv_hbm.1, ...), custom_call_target="tpu_custom_call" | custom-call | tf_op jit(solution)/shard_map/pallas_call | solution.py:697
  59.4 1.3 %copy.16 = bf16[2,8,512]{2,1,0:T(8,128)(2,1)} copy(bf16[2,8,512]{2,1,0:T(8,128)(2,1)} %shard_map.136) | data formatting | bytes 32768

commit v2 on v1

--- a/solution.py
+++ b/solution.py
@@ -269,9 +269,6 @@
     ssend,
     qsend,
     osend,
-    norm_s,
-    attn_s,
-    gain_s,
     load_sem,
     x_send_sem,
     x_recv_sem,
@@ -281,6 +278,7 @@
     q_recv_sem,
     o_send_sem,
     o_recv_sem,
+    o_pass_sem,
 ):
     f32, bf16 = jnp.float32, jnp.bfloat16
     hd, groups = HEAD_DIMENSION, KEY_VALUE_HEADS
@@ -290,6 +288,7 @@
     heads_here = q_cols // hd
     per_group = QUERY_HEADS // groups
     blocks = n // groups
+    span = 4
     cached_rows = ctx_dev * rows
     rank = qd_hbm.shape[1]
     me = lax.axis_index("tensor")
@@ -359,13 +358,8 @@
         lax.fori_loop(1, n, step, 0)
 
     def x_copy(t, slot, target):
-        size = xsend.shape[1] if t == 0 else chunks * rows
         return remote(
-            xsend.at[t, pl.ds(0, size)],
-            xg.at[t, slot, pl.ds(0, size)],
-            x_send_sem.at[t, target],
-            x_recv_sem.at[t, slot],
-            target,
+            xsend.at[t], xg.at[t, slot], x_send_sem.at[t, target], x_recv_sem.at[t, slot], target
         )
 
     def s_copy(t, slot, target):
@@ -378,6 +372,11 @@
             osend.at[t], og.at[t, slot], o_send_sem.at[t, target], o_recv_sem.at[t, slot], target
         )
 
+    def o_pass(t, slot, target):
+        return remote(
+            og.at[t, slot], og.at[t, slot], o_pass_sem.at[t, slot], o_recv_sem.at[t, slot], target
+        )
+
     def q_copy(t, slot, block, target):
         return remote(
             qsend.at[t], qg.at[t, slot], q_send_sem.at[t, block], q_recv_sem.at[t, slot], target
@@ -386,21 +385,15 @@
     lane = lax.broadcasted_iota(jnp.int32, (rows, hd), 1)
     row = lax.broadcasted_iota(jnp.int32, (rows, hd), 0)
     gains = gain_ref[...]
-    row16 = lax.broadcasted_iota(jnp.int32, (16, hd), 0)
 
     def split_chunks(x):
         return [x[:, c * hd : (c + 1) * hd] for c in range(x.shape[1] // hd)]
 
     current = current_ref[...].astype(f32)
-    gain16 = jnp.zeros((16, hd), f32)
-    for c, piece in enumerate(split_chunks(gains)):
-        gain16 = jnp.where(row16 == c, piece[0:1, :], gain16)
-
     def send_state(t):
-        parts = split_chunks(current) + ([gain16] if t == 0 else [])
-        message = jnp.concatenate(parts, axis=0).astype(bf16)
-        xsend[t, pl.ds(0, message.shape[0])] = message
-        xg[t, me, pl.ds(0, message.shape[0])] = message
+        message = jnp.concatenate(split_chunks(current * gains), axis=0).astype(bf16)
+        xsend[t] = message
+        xg[t, me] = message
         if t == 0:
             pl.semaphore_wait(barrier, n - 1)
         for_others(lambda target: x_copy(t, me, target).start())
@@ -461,7 +454,15 @@
     spread_column = lax.broadcasted_iota(jnp.int32, (rows, rows * rank), 1)
     spread_row = lax.broadcasted_iota(jnp.int32, (rows, rows * rank), 0)
     own_block = spread_column // rank == spread_row
-    even_block = lax.rem(lane // rank, 2) == 0
+    lane_block = lane // rank
+
+    def flip(index, bits):
+        bit = 1
+        while bit <= bits:
+            if bits & bit:
+                index = index + bit - 2 * bit * lax.rem(index // bit, 2)
+            bit *= 2
+        return index
 
     def contract(left, right):
         return lax.dot_general(
@@ -482,8 +483,11 @@
 
     def send_shrink(t):
         scaled = (current * gains).astype(bf16)
+        squares = jnp.sum(current * current, axis=1, keepdims=True)
         both = jnp.where(
-            even_block, fold(contract(scaled, dq_s[...])), fold(contract(scaled, dv_s[...]))
+            lane_block == 0,
+            fold(contract(scaled, dq_s[...])),
+            jnp.where(lane_block == 1, fold(contract(scaled, dv_s[...])), squares),
         )
         ssend[t] = both
         sg[t, me] = both
@@ -492,32 +496,29 @@
     send_shrink(0)
 
     for t in range(STEPS):
-        for_others(lambda source: x_copy(t, source, source).wait_recv())
-        squares = jnp.zeros((rows, hd), f32)
-        for d in range(n):
-            block = xg[t, d, pl.ds(0, chunks * rows)].astype(f32)
-            for c in range(chunks):
-                part = block[c * rows : (c + 1) * rows]
-                squares = squares + part * part
-            if t == 0:
-                gain_block = xg[0, d, pl.ds(chunks * rows, 16)].astype(f32)
-                gain_s[pl.ds(d * chunks, chunks)] = gain_block[0:chunks]
-        total = jnp.sum(squares, axis=1, keepdims=True)
-        inv_rms = lax.rsqrt(total / MODEL_WIDTH + eps_norm)
-        for d in range(n):
-            block = xg[t, d, pl.ds(0, chunks * rows)].astype(f32)
-            for c in range(chunks):
-                at = d * chunks + c
-                part = block[c * rows : (c + 1) * rows]
-                normed = part * inv_rms * gain_s[pl.ds(at, 1)]
-                norm_s[:, pl.ds(at * hd, hd)] = normed.astype(bf16)
+        if t == 0:
+            for copies in weights:
+                for copy in copies:
+                    copy.wait()
         products = jnp.zeros((rows, q_cols + 2 * kv_cols), f32)
-        for piece in range(pieces):
-            cols = pl.ds(piece * step_cols, step_cols)
-            if t == 0:
-                for copy in weights[piece]:
-                    copy.wait()
-            products = products + contract(norm_s[:, cols], w_s[:, cols])
+        for far in range(0, n, span):
+            first = flip(me, far) // span * span
+            parts = []
+            for k in range(span):
+                source = first + k
+                if far:
+                    x_copy(t, source, source).wait_recv()
+                else:
+
+                    @pl.when(source != me)
+                    def _():
+                        x_copy(t, source, source).wait_recv()
+
+                block = xg[t, source].astype(f32)
+                parts += [block[c * rows : (c + 1) * rows] for c in range(chunks)]
+            cols = pl.ds(pl.multiple_of(first * width, span * width), span * width)
+            state = jnp.concatenate(parts, axis=1).astype(bf16)
+            products = products + contract(state, w_s[:, cols])
         if t == 0:
             for copy in ups:
                 copy.wait()
@@ -529,15 +530,22 @@
         shrink = sg[t, 0]
         for d in range(1, n):
             shrink = shrink + sg[t, d]
+        squares = shrink[:, 2 * rank : 2 * rank + 1]
+        inv_rms = lax.rsqrt(squares / MODEL_WIDTH + eps_norm)
         shrink = shrink * inv_rms
-        turned = pltpu.roll(shrink, rank, 1)
-
-        def spread(x):
+
+        def spread(kind):
+            x = jnp.where(lane_block == kind, shrink, 0.0)
+            shift = rank
+            while shift < hd:
+                x = x + pltpu.roll(x, shift, 1)
+                shift *= 2
             x = jnp.concatenate([x] * (rows * rank // hd), axis=1)
             return jnp.where(own_block, x, 0.0).astype(bf16)
 
-        q_low = spread(jnp.where(even_block, shrink, turned))
-        v_low = spread(jnp.where(even_block, turned, shrink))
+        q_low = spread(0)
+        v_low = spread(1)
+        products = products * inv_rms
         q_up = jnp.dot(q_low, uq_s[...], preferred_element_type=f32)
         v_up = jnp.dot(v_low, uv_s[...], preferred_element_type=f32)
         query = products[:, :q_cols] + adapter_scale * q_up
@@ -609,10 +617,33 @@
         ).astype(bf16)
         osend[t] = message
         og[t, me] = message
-        for_others(lambda target: o_copy(t, me, target).start())
-        for_others(lambda source: o_copy(t, source, source).wait_recv())
-        for g in range(groups):
+        for k in range(2, n, 2):
+            o_copy(t, me, flip(me, k)).start()
+        sibling = flip(me, 1)
+        o_copy(t, me, sibling).start()
+        if t == 0:
+            for copy in out_weights:
+                copy.wait()
+        projected = jnp.zeros((rows, width), f32)
+        own_group = lax.rem(me, groups)
+        order = [k for k in range(groups) if k % 2 == 0] + [k for k in range(groups) if k % 2]
+        for k in order:
+            g = flip(own_group, k)
             found = []
+            for b in range(blocks):
+                source = b * groups + g
+                if k % 2:
+                    o_copy(t, source, source).wait_recv()
+                elif k:
+                    o_copy(t, source, source).wait_recv()
+                    o_pass(t, source, sibling).start()
+                else:
+
+                    @pl.when(source != me)
+                    def _():
+                        o_copy(t, source, source).wait_recv()
+                        o_pass(t, source, sibling).start()
+
             for b in range(blocks):
                 entry = og[t, b * groups + g].astype(f32)
                 packed = entry[per_group * rows : per_group * rows + rows]
@@ -629,18 +660,17 @@
             whole = shares[0]
             for share in shares[1:]:
                 whole = whole + share
+            shares = [share / whole for share in shares]
+            parts = []
             for h in range(per_group):
                 value = jnp.zeros((rows, hd), f32)
                 for share, (_, entry) in zip(shares, found):
-                    part = (share / whole)[:, h : h + 1]
-                    value = value + part * entry[h * rows : (h + 1) * rows]
-                attn_s[:, pl.ds((g * per_group + h) * hd, hd)] = value.astype(bf16)
-        projected = jnp.zeros((rows, width), f32)
-        for piece in range(pieces):
-            cols = pl.ds(piece * step_cols, step_cols)
-            if t == 0:
-                out_weights[piece].wait()
-            projected = projected + contract(attn_s[:, cols], wo_s[:, cols])
+                    value = value + share[:, h : h + 1] * entry[h * rows : (h + 1) * rows]
+                parts.append(value)
+            attention = jnp.concatenate(parts, axis=1).astype(bf16)
+            wide = per_group * hd
+            cols = pl.ds(pl.multiple_of(g * wide, wide), wide)
+            projected = projected + contract(attention, wo_s[:, cols])
         rounded = (current + projected).astype(bf16)
         out_ref[t] = rounded
         current = rounded.astype(f32)
@@ -651,7 +681,11 @@
     for t in range(STEPS):
         for_others(lambda target: x_copy(t, me, target).wait_send())
         for_others(lambda target: s_copy(t, me, target).wait_send())
-        for_others(lambda target: o_copy(t, me, target).wait_send())
+        for k in range(2, n, 2):
+            other = flip(me, k)
+            o_copy(t, me, other).wait_send()
+            o_pass(t, other, flip(me, 1)).wait_send()
+        o_copy(t, me, flip(me, 1)).wait_send()
         for block in range(blocks):
             target = me // 2 + block * groups
 
@@ -686,7 +720,7 @@
     per_group = QUERY_HEADS // KEY_VALUE_HEADS
     blocks = n // KEY_VALUE_HEADS
     kv_rows = ctx_dev * rows + 128
-    x_rows = chunks * rows + 16
+    x_rows = chunks * rows
     q_rows = (q_cols // hd + 2) * rows
     o_rows = per_group * rows + 16
     bf16, f32 = jnp.bfloat16, jnp.float32
@@ -720,9 +754,6 @@
             pltpu.VMEM((STEPS, rows, hd), f32),
             pltpu.VMEM((STEPS, q_rows, hd), bf16),
             pltpu.VMEM((STEPS, o_rows, hd), bf16),
-            pltpu.VMEM((rows, MODEL_WIDTH), bf16),
-            pltpu.VMEM((rows, QUERY_HEADS * hd), bf16),
-            pltpu.VMEM((MODEL_WIDTH // hd, hd), f32),
             dma((24,)),
             dma((STEPS, n)),
             dma((STEPS, n)),
@@ -730,6 +761,7 @@
             dma((STEPS, n)),
             dma((STEPS, blocks)),
             dma((STEPS, 2)),
+            dma((STEPS, n)),
             dma((STEPS, n)),
             dma((STEPS, n)),
         ],

time: 61.6 us -> 54.7 us (0.89)
  Pallas kernels: 58.1 us -> 51.7 us
    pallas_call x1, Pallas kernels: 58.1 us -> 51.7 us  [fused(): pl.pallas_call(functools.partial(fused_kernel, n, ctx_dev), out_shape=jax...]
where the time goes in v2:
time: 54.7 us; the launch traced here: 54.3 us
  Pallas kernels  51.7 us (95%)
  local copies, waits for them, and re-layouts  2.61 us (5%)
    pallas_call x1, Pallas kernels, fused(): pl.pallas_call(functools.partial(fused_kernel, n, ctx_dev), out_shape=jax...  51.7 us
    unnamed x1, local copies, waits for them, and re-layouts  1.32 us
    broadcast_in_dim x1, local copies, waits for them, and re-layouts, fused(): jnp.broadcast_to(attention_norm_gain.astype(f32)[None, :], (rows, width))  1.29 us

profile of v2, /device:TPU:0, one launch (start us, length us, event | category | flops | bytes accessed | tf_op | source)
XLA Modules:
  0.0 54.3 jit_solution(9433645584267193226)
XLA Ops:
  0.0 1.3 %broadcast_in_dim.2.gain_ref = f32[8,512]{1,0:T(8,128)} broadcast(bf16[512]{0:T(512)(128)(2,1)} %param.15), dimensions={1} | broadcast | bytes 17408 | tf_op jit(solution)/shard_map/broadcast_in_dim | solution.py:773
  1.3 51.7 %shard_map.136 = bf16[2,8,512]{2,1,0:T(8,128)(2,1)} custom-call(bf16[8,512]{1,0:T(8,128)(2,1)} %current_ref.1, f32[8,512]{1,0:T(8,128)} %broadcast_in_dim.2.gain_ref, s32[8]{0:T(128)} %adapter_ref.1, s32[8]{0:T(128)} %length_ref.1, bf16[512,8192]{1,0:T(8,128)(2,1)} %wq_hbm.1, bf16[64,8192]{1,0:T(8,128)(2,1)} %wk_hbm.1, bf16[64,8192]{1,0:T(8,128)(2,1)} %wv_hbm.1, ...), custom_call_target="tpu_custom_call" | custom-call | tf_op jit(solution)/shard_map/pallas_call | solution.py:731
  53.0 1.3 %copy.16 = bf16[2,8,512]{2,1,0:T(8,128)(2,1)} copy(bf16[2,8,512]{2,1,0:T(8,128)(2,1)} %shard_map.136) | data formatting | bytes 32768

commit v3 on v2

--- a/solution.py
+++ b/solution.py
@@ -263,17 +263,21 @@
     uv_s,
     xg,
     sg,
+    sp,
     qg,
     og,
     xsend,
     ssend,
+    ssum,
     qsend,
     osend,
     load_sem,
     x_send_sem,
     x_recv_sem,
+    x_pass_sem,
     s_send_sem,
     s_recv_sem,
+    s_pair_sem,
     q_send_sem,
     q_recv_sem,
     o_send_sem,
@@ -288,7 +292,6 @@
     heads_here = q_cols // hd
     per_group = QUERY_HEADS // groups
     blocks = n // groups
-    span = 4
     cached_rows = ctx_dev * rows
     rank = qd_hbm.shape[1]
     me = lax.axis_index("tensor")
@@ -350,21 +353,26 @@
             device_id_type=pl.DeviceIdType.MESH,
         )
 
-    def for_others(body):
-        def step(k, carry):
-            body(lax.rem(me + k, n))
-            return carry
-
-        lax.fori_loop(1, n, step, 0)
-
     def x_copy(t, slot, target):
         return remote(
             xsend.at[t], xg.at[t, slot], x_send_sem.at[t, target], x_recv_sem.at[t, slot], target
         )
 
+    def x_pass(t, slot, target):
+        return remote(
+            xg.at[t, slot], xg.at[t, slot], x_pass_sem.at[t, slot], x_recv_sem.at[t, slot], target
+        )
+
+    def s_pair(t):
+        return remote(ssend.at[t], sp.at[t], s_pair_sem.at[t, 0], s_pair_sem.at[t, 1], sibling)
+
     def s_copy(t, slot, target):
         return remote(
-            ssend.at[t], sg.at[t, slot], s_send_sem.at[t, target], s_recv_sem.at[t, slot], target
+            ssum.at[t],
+            sg.at[t, slot // 2],
+            s_send_sem.at[t, target // 2],
+            s_recv_sem.at[t, slot // 2],
+            target,
         )
 
     def o_copy(t, slot, target):
@@ -382,9 +390,18 @@
             qsend.at[t], qg.at[t, slot], q_send_sem.at[t, block], q_recv_sem.at[t, slot], target
         )
 
+    def flip(index, bits):
+        bit = 1
+        while bit <= bits:
+            if bits & bit:
+                index = index + bit - 2 * bit * lax.rem(index // bit, 2)
+            bit *= 2
+        return index
+
+    sibling = flip(me, 1)
     lane = lax.broadcasted_iota(jnp.int32, (rows, hd), 1)
     row = lax.broadcasted_iota(jnp.int32, (rows, hd), 0)
-    gains = gain_ref[...]
+    gains = jnp.broadcast_to(gain_ref[...].astype(f32)[None, :], (rows, width))
 
     def split_chunks(x):
         return [x[:, c * hd : (c + 1) * hd] for c in range(x.shape[1] // hd)]
@@ -396,14 +413,15 @@
         xg[t, me] = message
         if t == 0:
             pl.semaphore_wait(barrier, n - 1)
-        for_others(lambda target: x_copy(t, me, target).start())
+        for k in (*range(2, n, 2), 1):
+            x_copy(t, me, flip(me, k)).start()
 
     send_state(0)
 
     lengths = jnp.zeros((rows, hd), jnp.int32)
     for r in range(rows):
         lengths = jnp.where(row == r, length_ref[r], lengths)
-    lane_even = lax.rem(lane, 2) == 0
+    lane_even = (lane & 1) == 0
 
     def angle_tables(pair, positions):
         frequency = jnp.exp(pair.astype(f32) * jnp.float32(-2.0 * math.log(theta_base) / hd))
@@ -411,7 +429,7 @@
         sine = jnp.sin(angles)
         return jnp.cos(angles), jnp.where(lane_even, -sine, sine)
 
-    fresh_pair = lax.rem(me, 2) * (kv_cols // 2) + lax.rem(lane, kv_cols) // 2
+    fresh_pair = lax.rem(me, 2) * (kv_cols // 2) + (lane & (kv_cols - 1)) // 2
     is_key = lane < kv_cols
     tables = []
     for t in range(STEPS):
@@ -438,11 +456,11 @@
         wide_length = jnp.where(wide_row == r, length_ref[r], wide_length)
     own_cached = (
         (column < cached_rows)
-        & (lax.rem(column, rows) == wide_row)
-        & (seq_block * ctx_dev + column // rows < wide_length)
+        & ((column & (rows - 1)) == wide_row)
+        & (seq_block * cached_rows + column < wide_length * rows)
     )
     fresh_column = column - cached_rows
-    fresh_row = (fresh_column >= 0) & (lax.rem(column, 16) == wide_row) & (seq_block == 0)
+    fresh_row = (fresh_column >= 0) & ((column & 15) == wide_row) & (seq_block == 0)
 
     for copy in small:
         copy.wait()
@@ -455,14 +473,6 @@
     spread_row = lax.broadcasted_iota(jnp.int32, (rows, rows * rank), 0)
     own_block = spread_column // rank == spread_row
     lane_block = lane // rank
-
-    def flip(index, bits):
-        bit = 1
-        while bit <= bits:
-            if bits & bit:
-                index = index + bit - 2 * bit * lax.rem(index // bit, 2)
-            bit *= 2
-        return index
 
     def contract(left, right):
         return lax.dot_general(
@@ -490,8 +500,7 @@
             jnp.where(lane_block == 1, fold(contract(scaled, dv_s[...])), squares),
         )
         ssend[t] = both
-        sg[t, me] = both
-        for_others(lambda target: s_copy(t, me, target).start())
+        s_pair(t).start()
 
     send_shrink(0)
 
@@ -501,24 +510,30 @@
                 for copy in copies:
                     copy.wait()
         products = jnp.zeros((rows, q_cols + 2 * kv_cols), f32)
-        for far in range(0, n, span):
-            first = flip(me, far) // span * span
-            parts = []
-            for k in range(span):
-                source = first + k
-                if far:
-                    x_copy(t, source, source).wait_recv()
-                else:
-
-                    @pl.when(source != me)
-                    def _():
-                        x_copy(t, source, source).wait_recv()
-
-                block = xg[t, source].astype(f32)
-                parts += [block[c * rows : (c + 1) * rows] for c in range(chunks)]
-            cols = pl.ds(pl.multiple_of(first * width, span * width), span * width)
-            state = jnp.concatenate(parts, axis=1).astype(bf16)
-            products = products + contract(state, w_s[:, cols])
+
+        def project(source):
+            block = xg[t, source].astype(f32)
+            parts = [block[c * rows : (c + 1) * rows] for c in range(chunks)]
+            cols = pl.ds(pl.multiple_of(source * width, width), width)
+            return contract(jnp.concatenate(parts, axis=1).astype(bf16), w_s[:, cols])
+
+        for k in range(0, n, 2):
+            source = flip(me, k)
+            if k:
+                x_copy(t, source, source).wait_recv()
+                x_pass(t, source, sibling).start()
+            products = products + project(source)
+            if k == 2:
+                s_pair(t).wait_recv()
+                pair_sum = ssend[t] + sp[t]
+                ssum[t] = pair_sum
+                sg[t, me // 2] = pair_sum
+                for other in range(2, n, 2):
+                    s_copy(t, me, flip(me, other)).start()
+        for k in range(1, n, 2):
+            source = flip(me, k)
+            x_copy(t, source, source).wait_recv()
+            products = products + project(source)
         if t == 0:
             for copy in ups:
                 copy.wait()
@@ -526,9 +541,11 @@
                 adapter = adapter_ref[r]
                 uq_s[pl.ds(r * rank, rank)] = qu_s[adapter]
                 uv_s[pl.ds(r * rank, rank)] = vu_s[adapter]
-        for_others(lambda source: s_copy(t, source, source).wait_recv())
+        for k in range(2, n, 2):
+            source = flip(me, k)
+            s_copy(t, source, source).wait_recv()
         shrink = sg[t, 0]
-        for d in range(1, n):
+        for d in range(1, n // 2):
             shrink = shrink + sg[t, d]
         squares = shrink[:, 2 * rank : 2 * rank + 1]
         inv_rms = lax.rsqrt(squares / MODEL_WIDTH + eps_norm)
@@ -619,7 +636,6 @@
         og[t, me] = message
         for k in range(2, n, 2):
             o_copy(t, me, flip(me, k)).start()
-        sibling = flip(me, 1)
         o_copy(t, me, sibling).start()
         if t == 0:
             for copy in out_weights:
@@ -679,13 +695,16 @@
             send_shrink(t + 1)
 
     for t in range(STEPS):
-        for_others(lambda target: x_copy(t, me, target).wait_send())
-        for_others(lambda target: s_copy(t, me, target).wait_send())
+        x_copy(t, me, sibling).wait_send()
+        s_pair(t).wait_send()
         for k in range(2, n, 2):
             other = flip(me, k)
+            x_copy(t, me, other).wait_send()
+            x_pass(t, other, sibling).wait_send()
+            s_copy(t, me, other).wait_send()
             o_copy(t, me, other).wait_send()
-            o_pass(t, other, flip(me, 1)).wait_send()
-        o_copy(t, me, flip(me, 1)).wait_send()
+            o_pass(t, other, sibling).wait_send()
+        o_copy(t, me, sibling).wait_send()
         for block in range(blocks):
             target = me // 2 + block * groups
 
@@ -747,10 +766,12 @@
             pltpu.VMEM((rows * rank, q_cols), bf16),
             pltpu.VMEM((rows * rank, kv_cols), bf16),
             pltpu.VMEM((STEPS, n, x_rows, hd), bf16),
-            pltpu.VMEM((STEPS, n, rows, hd), f32),
+            pltpu.VMEM((STEPS, n // 2, rows, hd), f32),
+            pltpu.VMEM((STEPS, rows, hd), f32),
             pltpu.VMEM((STEPS, 2, q_rows, hd), bf16),
             pltpu.VMEM((STEPS, n, o_rows, hd), bf16),
             pltpu.VMEM((STEPS, x_rows, hd), bf16),
+            pltpu.VMEM((STEPS, rows, hd), f32),
             pltpu.VMEM((STEPS, rows, hd), f32),
             pltpu.VMEM((STEPS, q_rows, hd), bf16),
             pltpu.VMEM((STEPS, o_rows, hd), bf16),
@@ -758,7 +779,9 @@
             dma((STEPS, n)),
             dma((STEPS, n)),
             dma((STEPS, n)),
-            dma((STEPS, n)),
+            dma((STEPS, n // 2)),
+            dma((STEPS, n // 2)),
+            dma((STEPS, 2)),
             dma((STEPS, blocks)),
             dma((STEPS, 2)),
             dma((STEPS, n)),
@@ -770,7 +793,7 @@
         ),
     )(
         residual_input,
-        jnp.broadcast_to(attention_norm_gain.astype(f32)[None, :], (rows, width)),
+        attention_norm_gain,
         request_adapter,
         cached_lengths,
         wq,

time: 54.7 us -> 53.2 us (0.973)
  local copies, waits for them, and re-layouts: 2.61 us -> 1.32 us
    broadcast_in_dim x1 -> x0, local copies, waits for them, and re-layouts: 1.29 us -> none  [fused(): jnp.broadcast_to(attention_norm_gain.astype(f32)[None, :], (rows, width))]
where the time goes in v3:
time: 53.2 us; the launch traced here: 52.9 us
  Pallas kernels  51.6 us (97%)
  local copies, waits for them, and re-layouts  1.32 us (2%)
    pallas_call x1, Pallas kernels, fused(): pl.pallas_call(functools.partial(fused_kernel, n, ctx_dev), out_shape=jax...  51.6 us
    unnamed x1, local copies, waits for them, and re-layouts  1.32 us

profile of v3, /device:TPU:0, one launch (start us, length us, event | category | flops | bytes accessed | tf_op | source)
XLA Modules:
  0.0 52.9 jit_solution(1316604022312099670)
XLA Ops:
  0.0 51.6 %shard_map.136 = bf16[2,8,512]{2,1,0:T(8,128)(2,1)} custom-call(bf16[8,512]{1,0:T(8,128)(2,1)} %current_ref.1, bf16[512]{0:T(512)(128)(2,1)} %gain_ref.1, s32[8]{0:T(128)} %adapter_ref.1, s32[8]{0:T(128)} %length_ref.1, bf16[512,8192]{1,0:T(8,128)(2,1)} %wq_hbm.1, bf16[64,8192]{1,0:T(8,128)(2,1)} %wk_hbm.1, bf16[64,8192]{1,0:T(8,128)(2,1)} %wv_hbm.1, ...), custom_call_target="tpu_custom_call" | custom-call | tf_op jit(solution)/shard_map/pallas_call | solution.py:750
  51.6 1.3 %copy.16 = bf16[2,8,512]{2,1,0:T(8,128)(2,1)} copy(bf16[2,8,512]{2,1,0:T(8,128)(2,1)} %shard_map.136) | data formatting | bytes 32768
